TPU v7x, 32 devices: a whole 2x2x4 slice. The times are simulated.
32 devices in a mesh: groups: 2 (over x), tensor: 2 (over core), replica: 8 (over z, y).
Axes of the slice: x: 2, y: 2, z: 4, core: 2. Of those that a mesh axis runs over, the one named last changes fastest.
Arguments:
- hidden: bfloat16 [512, 8192], P(('groups', 'replica'), 'tensor'), parts along dimension 0, may hold values from -6 to 6
- base_query_rows: bfloat16 [512, 4096], P(('groups', 'replica'), 'tensor'), parts along dimension 0, may hold values from -110 to 110
- adapter_down_weight: bfloat16 [128, 8192, 64], P(('groups', 'replica'), 'tensor'), parts along dimension 0, may hold values from -0.0625 to 0.0625
- adapter_up_weight: bfloat16 [128, 64, 4096], P(('groups', 'replica'), None, 'tensor'), parts along dimension 0, may hold values from -0.75 to 0.75
- request_adapter: int32 [512], P(('groups', 'replica')), parts along dimension 0, may hold values from 0 to 63, as said below
- adapter_pool_row: int32 [128], P('groups'), parts along dimension 0, may hold values from 0 to 63, as said below
- cached_keys: bfloat16 [512, 192, 512], P(('groups', 'replica'), None, 'tensor'), parts along dimension 0, may hold values from -5 to 5
- cached_values: bfloat16 [512, 192, 512], P(('groups', 'replica'), None, 'tensor'), parts along dimension 0, may hold values from -6 to 6
- request_cache_lengths: int32 [512], P(('groups', 'replica')), parts along dimension 0, may hold values from 48 to 192, as said below
Outputs:
- attended: bfloat16 [512, 4096], P(('groups', 'replica'), 'tensor'), parts along dimension 0
There are 2 independent parts, one for each index of `groups`. A program takes and returns all parts, laid end to end along the dimension named above; each array names one. Nothing has to cross between parts.
Inputs may be any that keep to these rules, and one draw needn't show every extreme that they name: A permutation: adapter a's matrices are row adapter_pool_row[a] of adapter_down_weight and adapter_up_weight. `request_adapter`: in each aligned block of 32 requests, at most 8 requests name adapters whose pool rows lie in one run k * 8 to (k + 1) * 8 - 1; in every block some run is named by exactly 8 requests. `request_cache_lengths`: every aligned block of 32 requests holds a request of 192 positions.
All inputs are finite; a program needn't handle non-finite values.
Results may differ from a plain program's by a relative error of at most 0.0075.
Values may be sent and summed in bfloat16 or wider, within the bound.
A program may use at most 64 MiB of HBM per device.

v0:
```python
import jax
import jax.numpy as jnp
from jax import lax
from jax.sharding import PartitionSpec as P

HEAD_WIDTH = 128


def attend_rows(query_rows, key_rows, value_rows, request_cache_lengths, head_size):
    row_total, cache_size, kv_width = key_rows.shape
    kv_count = kv_width // head_size
    group_size = query_rows.shape[1] // kv_width
    query_heads = query_rows.reshape(row_total, kv_count, group_size, head_size)
    key_heads = key_rows.reshape(row_total, cache_size, kv_count, head_size)
    value_heads = value_rows.reshape(row_total, cache_size, kv_count, head_size)
    scores = jnp.einsum(
        "rkgd,rlkd->rkgl", query_heads, key_heads, preferred_element_type=jnp.float32
    ) * head_size ** (-0.5)
    positions = jnp.arange(cache_size, dtype=jnp.int32)
    valid = positions[None, :] < request_cache_lengths[:, None]
    scores = jnp.where(valid[:, None, None, :], scores, jnp.float32(-1e30))
    row_max = jnp.max(scores, axis=-1, keepdims=True)
    expo = jnp.exp(scores - row_max)
    totals = jnp.sum(expo, axis=-1, keepdims=True)
    weights = (expo / totals).astype(jnp.bfloat16)
    result = jnp.einsum("rkgl,rlkd->rkgd", weights, value_heads, preferred_element_type=jnp.float32)
    return result.astype(jnp.bfloat16).reshape(row_total, kv_count * group_size * head_size)


def masked_down_output(input_rows, local_pool_row, adapter_down_weight):
    holding_count, input_width, adapter_rank_width = adapter_down_weight.shape
    partial_value_sum = jnp.einsum(
        "vk,lkb->vlb", input_rows, adapter_down_weight, preferred_element_type=jnp.float32
    )
    partial_value_sum = partial_value_sum.reshape(
        input_rows.shape[0], holding_count * adapter_rank_width
    )
    column_index = (
        jnp.arange(holding_count * adapter_rank_width, dtype=jnp.int32) // adapter_rank_width
    )
    keep_mask = column_index[None, :] == local_pool_row[:, None]
    return jnp.where(keep_mask, partial_value_sum, 0.0)


def local(
    hidden,
    base_query_rows,
    adapter_down_weight,
    adapter_up_weight,
    request_adapter,
    adapter_pool_row,
    cached_keys,
    cached_values,
    request_cache_lengths,
):
    holding_count, adapter_rank_width, output_width = adapter_up_weight.shape
    flattened_up_weight = adapter_up_weight.reshape(
        holding_count * adapter_rank_width, output_width
    )
    id_table = jnp.arange(adapter_pool_row.shape[0], dtype=jnp.int32)
    id_hits = request_adapter[:, None] == id_table[None, :]
    pool_index = jnp.sum(jnp.where(id_hits, adapter_pool_row[None, :], 0), axis=1)
    every_request_row, every_index = (
        lax.all_gather(hidden, "replica", axis=0, tiled=True),
        lax.all_gather(pool_index, "replica", axis=0, tiled=True),
    )
    my_index = lax.axis_index("replica")
    local_pool_row = jnp.where(
        every_index // holding_count == my_index, every_index % holding_count, -1
    )
    partial_value_sum = masked_down_output(every_request_row, local_pool_row, adapter_down_weight)
    shrink = lax.psum(partial_value_sum, "tensor").astype(jnp.bfloat16)
    delta_rows = lax.psum_scatter(
        jnp.dot(shrink, flattened_up_weight, preferred_element_type=jnp.float32).astype(
            jnp.bfloat16
        ),
        "replica",
        scatter_dimension=0,
        tiled=True,
    )
    query_rows = (base_query_rows.astype(jnp.float32) + delta_rows.astype(jnp.float32)).astype(
        jnp.bfloat16
    )
    return attend_rows(query_rows, cached_keys, cached_values, request_cache_lengths, HEAD_WIDTH)


def solution(mesh):
    return jax.shard_map(
        local,
        mesh=mesh,
        in_specs=(
            P(("groups", "replica"), "tensor"),
            P(("groups", "replica"), "tensor"),
            P(("groups", "replica"), "tensor", None),
            P(("groups", "replica"), None, "tensor"),
            P(("groups", "replica")),
            P("groups"),
            P(("groups", "replica"), None, "tensor"),
            P(("groups", "replica"), None, "tensor"),
            P(("groups", "replica")),
        ),
        out_specs=P(("groups", "replica"), "tensor"),
        check_vma=False,
    )
```

profile of v0, /device:TPU:0, one launch (start us, length us, event | category | flops | bytes accessed | tf_op | source)
XLA Modules:
  0.0 152.1 jit_solution(14475724656638234346)
XLA Ops:
  6.5 0.0 copy-start
  6.5 0.0 all-gather.2.cloned.1.call-start
  6.5 0.7 all-gather.2.cloned.1.call-update
  7.3 0.0 reduce-scatter.2.cloned.1.call-start
  7.3 1.4 dynamic-slice
  9.4 0.9 select_reduce_fusion
  10.2 0.2 dynamic-update-slice
  10.5 13.2 %all-reduce = s32[256]{0:T(256)S(1)} all-reduce(s32[256]{0:T(256)S(1)} %dynamic-update-slice), channel_id=1, replica_groups=mesh['groups'=2,'tensor'=2,'replica'=8] {'replica'}, use_global_device_ids=true, to_apply=%add | all-reduce | flops 256 | bytes 2048
  23.6 37.9 %all-gather.2.cloned.1.call-done = bf16[256,4096]{1,0:T(8,128)(2,1)} async-done(((bf16[32,4096]{1,0:T(8,128)(2,1)}), bf16[256,4096]{1,0:T(8,128)(2,1)}) %all-gather.2.cloned.1.call-update) | async-done | bytes 2097168 | tf_op jit(solution)/shard_map/all_gather | solution.py:64
  61.5 4.9 %fusion.15 = f32[256,512]{0,1:T(8,128)} fusion(bf16[256,4096]{1,0:T(8,128)(2,1)} %all-gather.2.cloned.1.call-done, bf16[4096,512]{0,1:T(8,128)(2,1)} %bitcast.51, s32[256]{0:T(256)S(1)} %compare_select_fusion, s32[512]{0:T(512)S(1)} %add_select_fusion), kind=kOutput, calls=%fused_computation.13 | convolution fusion | flops 1074003968 | bytes 6818816
  66.4 0.0 copy-start.2
  66.4 0.0 copy-start.1
  66.4 5.7 %all-reduce.2 = bf16[256,512]{0,1:T(8,128)(2,1)S(1)} all-reduce(f32[256,512]{0,1:T(8,128)} %fusion.15), channel_id=1, replica_groups=mesh['groups'=2,'tensor'=2,'replica'=8] {'tensor'}, use_global_device_ids=true, to_apply=%region_1.2 | all-reduce | flops 131072 | bytes 786432 | tf_op jit(solution)/shard_map/psum | solution.py:72
  72.1 3.3 %convolution_convert_fusion = bf16[256,2048]{1,0:T(8,128)(2,1)} fusion(bf16[512,2048]{1,0:T(8,128)(2,1)} %bitcast.48, bf16[256,512]{0,1:T(8,128)(2,1)S(1)} %all-reduce.2), kind=kOutput, calls=%fused_computation.7 | convolution fusion | flops 537395200 | bytes 3407872 | tf_op jit(solution)/shard_map/dot_general | solution.py:74
  75.5 0.0 reduce-scatter.2.cloned.1.call-update
  75.5 0.0 copy-done.2
  75.5 0.1 iota_compare_fusion
  75.6 62.3 %reduce-scatter.2.cloned.1.call-done = bf16[32,2048]{1,0:T(8,128)(2,1)} async-done(((bf16[256,2048]{1,0:T(8,128)(2,1)}), bf16[32,2048]{1,0:T(8,128)(2,1)}) %reduce-scatter.2.cloned.1.call-update) | async-done | bytes 131088 | tf_op jit(solution)/shard_map/reduce_scatter | solution.py:73
  137.9 0.0 copy-done.1
  137.9 0.9 fusion.21
  138.9 0.0 copy-done
  138.9 2.6 %fusion.25 = (f32[32,2,8]{2,1,0:T(2,128)S(1)}, f32[32,2,8,192]{3,2,1,0:T(8,128)}) fusion(bf16[32,2,8,128]{3,2,1,0:T(8,128)(2,1)S(1)} %bitcast.49, pred[32,192]{1,0:T(8,128)(4,1)S(1)} %iota_compare_fusion, bf16[32,192,256]{2,1,0:T(8,128)(2,1)S(1)} %copy-done), kind=kOutput, calls=%fused_computation.37 | convolution fusion | flops 25559232 | bytes 3678208 | tf_op jit(solution)/shard_map/sub | solution.py:23
  141.5 3.0 %fusion.16 = bf16[32,2,8,128]{3,2,1,0:T(8,128)(2,1)S(1)} fusion(f32[32,2,8,192]{3,2,1,0:T(8,128)} %get-tuple-element.6, f32[32,2,8]{2,1,0:T(2,128)S(1)} %get-tuple-element.5, bf16[32,192,256]{2,1,0:T(8,128)(2,1)} %param.16), kind=kOutput, calls=%fused_computation.14 | convolution fusion | flops 25427968 | bytes 3672064 | tf_op jit(solution)/shard_map/rkgl,rlkd->rkgd/dot_general | solution.py:26
  144.6 0.7 copy.35
  (4 shorter events, 0.0 us)
Async XLA Ops:
  6.5 132.3 %copy-start = (bf16[32,192,256]{2,1,0:T(8,128)(2,1)S(1)}, bf16[32,192,256]{2,1,0:T(8,128)(2,1)}, u32[]{:S(2)}) copy-start(bf16[32,192,256]{2,1,0:T(8,128)(2,1)} %param.15) | copy-start | bytes 9437188
  6.5 55.0 %all-gather.2.cloned.1.call-start = ((), (), s32[]{:S(2)}) async-start(), calls=%async_computation.1 | async-start | bytes 2359296 | tf_op jit(solution)/shard_map/all_gather | solution.py:64
  7.3 130.6 %reduce-scatter.2.cloned.1.call-start = ((), (), s32[]{:S(2)}) async-start(), calls=%async_computation.2 | async-start | bytes 1179648 | tf_op jit(solution)/shard_map/reduce_scatter | solution.py:73
  66.4 9.1 %copy-start.2 = (s32[32]{0:T(128)S(1)}, s32[32]{0:T(128)}, u32[]{:S(2)}) copy-start(s32[32]{0:T(128)} %param.17) | copy-start | bytes 388
  66.4 71.5 %copy-start.1 = (bf16[32,2048]{1,0:T(8,128)(2,1)S(1)}, bf16[32,2048]{1,0:T(8,128)(2,1)}, u32[]{:S(2)}) copy-start(bf16[32,2048]{1,0:T(8,128)(2,1)} %param.10) | copy-start | bytes 393220
Sparse Core Ops, SparseCore 0:
  9.5 51.9 all-gather.1
  75.6 62.2 reduce-scatter.1
where the time goes:
time: 152 us
  waiting for transfers between devices  101 us (66%)
  blocking collectives  18.9 us (12%)
  between operations  14.1 us (9%)
  matrix products  13.9 us (9%)
  local copies, waits for them, and re-layouts  2.38 us (2%)
  other arithmetic  1.88 us (1%)
    reduce_scatter x1, waiting for transfers between devices, local(): lax.psum_scatter(jnp.dot(shrink, flattened_up_weight, preferred_element_t...  62.3 us
    all_gather x1, waiting for transfers between devices, local(): lax.all_gather(hidden, 'replica', axis=0, tiled=True)  37.9 us
    unnamed x1, blocking collectives  13.2 us
    psum x1, blocking collectives, local(): shrink = lax.psum(partial_value_sum, 'tensor').astype(jnp.bfloat16)  5.72 us
    unnamed x1, matrix products  4.9 us
    dot_general x1, matrix products, local(): jnp.dot(shrink, flattened_up_weight, preferred_element_type=jnp.float32)  3.32 us
  transfers between devices with their start and end apart: 2, of which 2 were waited for; matrix products, arithmetic and copies ran while one was open for 2% of the time, Pallas kernels for 0%

commit v1 on v0

v1 whole, which is shorter than its diff:
```python
import functools

import jax
import jax.numpy as jnp
from jax import lax
from jax.experimental import pallas as pl
from jax.experimental.pallas import tpu as pltpu
from jax.sharding import PartitionSpec as P

HEAD_WIDTH = 128
TILE = 16
LANES = 128
F32 = jnp.float32
BF16 = jnp.bfloat16


def iota(shape, axis):
    return lax.broadcasted_iota(jnp.int32, shape, axis)


def to_column(row, size):
    square = iota((size, size), 0) == iota((size, size), 1)
    return jnp.sum(jnp.where(square, row, 0), axis=1, keepdims=True)


def to_row(column, size):
    square = iota((size, size), 0) == iota((size, size), 1)
    return jnp.sum(jnp.where(square, column, 0), axis=0, keepdims=True)


def kernel(
    replicas, holding, rank_width,
    hidden_ref, base_ref, adapter_ref, pool_ref, length_ref,
    down_hbm, up_hbm, key_hbm, value_hbm,
    out_ref,
    down, up, keys, values, send_rows, got_rows, part, other_part,
    send_delta, got_delta, query,
    load_sem, row_send, row_recv, part_sem, delta_send, delta_recv,
):
    rows, width = hidden_ref.shape
    out_width = up.shape[1]
    cap = 2 * rows // replicas
    pieces = TILE // cap
    slots = replicas * TILE
    piece_width = width // pieces
    delta_width = out_width // pieces
    me = lax.axis_index("replica")
    core = lax.axis_index("tensor")

    loads = [
        pltpu.make_async_copy(src, dst, load_sem.at[at])
        for at, (src, dst) in enumerate(
            ((down_hbm, down), (up_hbm, up), (key_hbm, keys), (value_hbm, values))
        )
    ]
    barrier = pltpu.get_barrier_semaphore()
    for off in range(1, replicas):
        pl.semaphore_signal(
            barrier, inc=1, device_id={"replica": lax.rem(me + off, replicas)},
            device_id_type=pl.DeviceIdType.MESH,
        )
    pl.semaphore_signal(
        barrier, inc=1, device_id={"tensor": 1 - core}, device_id_type=pl.DeviceIdType.MESH
    )
    for load in loads:
        load.start()

    adapter_col = to_column(adapter_ref[...], rows)
    pool_row = pool_ref[...]
    pool_size = pool_row.shape[1]
    hits = adapter_col == iota((rows, pool_size), 1)
    index_col = jnp.sum(jnp.where(hits, pool_row, 0), axis=1, keepdims=True)
    owner_col = index_col // holding
    local_col = index_col - owner_col * holding
    owner_row = to_row(owner_col, rows)
    local_row = to_row(local_col, rows)
    same = owner_col == owner_row
    before_i = iota((rows, rows), 1) < iota((rows, rows), 0)
    before_j = iota((rows, rows), 0) < iota((rows, rows), 1)
    place_col = jnp.sum(jnp.where(same & before_i, 1, 0), axis=1, keepdims=True)
    place_row = jnp.sum(jnp.where(same & before_j, 1, 0), axis=0, keepdims=True)

    at_row = iota((slots, rows), 0)
    pick = (owner_row == at_row // TILE) & (place_row == at_row % cap)
    pick_bf = jnp.where(pick, 1.0, 0.0).astype(BF16)
    local_slot = jnp.sum(jnp.where(pick, local_row + 1, 0), axis=1, keepdims=True) - 1
    piece_of = (iota((slots, 1), 0) % TILE) // cap

    step = min(piece_width, 512)
    for start in range(0, piece_width, step):
        taken = None
        for h in range(pieces):
            found = jnp.dot(
                pick_bf, hidden_ref[:, h * piece_width + start:h * piece_width + start + step],
                preferred_element_type=F32,
            )
            taken = found if taken is None else jnp.where(piece_of == h, found, taken)
        send_rows[:, :, start:start + step] = taken.astype(BF16).reshape(replicas, TILE, step)
    send_rows[:, :, piece_width:] = jnp.broadcast_to(
        local_slot.astype(F32), (slots, LANES)
    ).astype(BF16).reshape(replicas, TILE, LANES)

    pl.semaphore_wait(barrier, replicas)

    def exchange(source, target, send_sem, recv_sem):
        copies = []
        order = sorted(range(1, replicas), key=lambda off: abs(off - replicas // 2))
        for off in order:
            there = lax.rem(me + off, replicas)
            copy = pltpu.make_async_remote_copy(
                src_ref=source.at[there], dst_ref=target.at[me],
                send_sem=send_sem.at[off], recv_sem=recv_sem.at[off],
                device_id={"replica": there}, device_id_type=pl.DeviceIdType.MESH,
            )
            copy.start()
            copies.append(copy)
        return copies

    row_copies = exchange(send_rows, got_rows, row_send, row_recv)
    got_rows[me] = send_rows[me]
    loads[0].wait()
    for copy in row_copies:
        copy.wait()

    partial_sum = None
    for h in range(pieces):
        term = lax.dot_general(
            got_rows[:, :, :piece_width].reshape(slots, piece_width),
            down[:, h * piece_width:(h + 1) * piece_width],
            (((1,), (1,)), ((), ())), preferred_element_type=F32,
        )
        partial_sum = term if partial_sum is None else jnp.where(piece_of == h, term, partial_sum)
    local = got_rows[:, :, piece_width:].reshape(slots, LANES).astype(F32)
    per_tile = LANES // rank_width
    tiles = holding * rank_width // LANES
    lane_adapter = (iota((slots, LANES), 1) // rank_width).astype(F32)
    folded = jnp.zeros((slots, LANES), F32)
    for tile in range(tiles):
        keep = local == lane_adapter + tile * per_tile
        folded += jnp.where(keep, partial_sum[:, tile * LANES:(tile + 1) * LANES], 0.0)
    shift = rank_width
    while shift < LANES:
        folded = folded + pltpu.roll(folded, shift, 1)
        shift *= 2
    shift = cap
    row_at = iota((slots, 1), 0)
    while shift < TILE:
        upper = (row_at // shift) % 2 == 1
        folded = folded + jnp.where(
            upper, pltpu.roll(folded, shift, 0), pltpu.roll(folded, slots - shift, 0)
        )
        shift *= 2
    part[...] = folded
    swap = pltpu.make_async_remote_copy(
        src_ref=part, dst_ref=other_part, send_sem=part_sem.at[0], recv_sem=part_sem.at[1],
        device_id={"tensor": 1 - core}, device_id_type=pl.DeviceIdType.MESH,
    )
    swap.start()
    loads[1].wait()
    swap.wait()
    shrink = (part[...] + other_part[...]).astype(BF16).astype(F32)
    wide = jnp.concatenate(
        [
            jnp.where(local == lane_adapter + tile * per_tile, shrink, 0.0).astype(BF16)
            for tile in range(tiles)
        ],
        axis=1,
    )
    step = min(delta_width, 512)
    for start in range(0, delta_width, step):
        taken = None
        for h in range(pieces):
            found = jnp.dot(
                wide, up[:, h * delta_width + start:h * delta_width + start + step],
                preferred_element_type=F32,
            )
            taken = found if taken is None else jnp.where(piece_of == h, found, taken)
        send_delta[:, :, start:start + step] = taken.astype(BF16).reshape(replicas, TILE, step)
    delta_copies = exchange(send_delta, got_delta, delta_send, delta_recv)
    got_delta[me] = send_delta[me]

    at_col = iota((rows, slots), 1)
    mine = (owner_col == at_col // TILE) & (place_col == at_col % cap)
    back = [
        jnp.where(mine & ((at_col % TILE) // cap == h), 1.0, 0.0).astype(BF16)
        for h in range(pieces)
    ]
    loads[2].wait()
    loads[3].wait()
    for copy in delta_copies:
        copy.wait()
    for h in range(pieces):
        columns = slice(h * delta_width, (h + 1) * delta_width)
        delta = jnp.dot(
            back[h], got_delta[...].reshape(slots, delta_width), preferred_element_type=F32
        )
        query[:, columns] = (base_ref[:, columns].astype(F32) + delta).astype(BF16).astype(F32)

    cache_len, kv_width = keys.shape[1:]
    kv_heads = kv_width // HEAD_WIDTH
    heads = out_width // HEAD_WIDTH
    group = heads // kv_heads
    block = 8
    tall = heads * block
    request_of = iota((tall, 1), 0) % block
    kv_of_row = iota((tall, 1), 0) // (group * block)
    length_col = to_column(length_ref[...], rows)
    position = iota((block, cache_len), 1)

    def attend(first):
        loaded = query[first:first + block, :]
        stacked = jnp.concatenate(
            [loaded[:, at * HEAD_WIDTH:(at + 1) * HEAD_WIDTH] for at in range(heads)], axis=0
        )
        spread = jnp.concatenate(
            [jnp.where(kv_of_row == kv, stacked, 0.0).astype(BF16) for kv in range(kv_heads)],
            axis=1,
        )
        scores = None
        for at in range(block):
            found = lax.dot_general(
                spread, keys[first + at], (((1,), (1,)), ((), ())), preferred_element_type=F32
            )
            scores = found if scores is None else jnp.where(request_of == at, found, scores)
        valid = position < length_col[first:first + block, :]
        bias = jnp.where(valid, 0.0, -1e30).astype(F32)
        valid_all = jnp.concatenate([bias] * heads, axis=0)
        scores = jnp.where(valid_all < 0.0, -1e30, scores * (HEAD_WIDTH ** -0.5))
        expo = jnp.exp(scores - jnp.max(scores, axis=1, keepdims=True))
        weights = expo / jnp.sum(expo, axis=1, keepdims=True)
        total = jnp.zeros((tall, kv_width), F32)
        for at in range(block):
            chosen = jnp.where(request_of == at, weights, 0.0).astype(BF16)
            total += jnp.dot(chosen, values[first + at], preferred_element_type=F32)
        return [
            total[at * block:(at + 1) * block,
                  (at // group) * HEAD_WIDTH:(at // group + 1) * HEAD_WIDTH]
            for at in range(heads)
        ]

    for first in range(0, rows, 2 * block):
        low, high = attend(first), attend(first + block)
        for at in range(heads):
            out_ref[first:first + 2 * block, at * HEAD_WIDTH:(at + 1) * HEAD_WIDTH] = (
                jnp.concatenate([low[at], high[at]], axis=0).astype(BF16)
            )


def local_step(
    replicas, hidden, base, down, up, request_adapter, adapter_pool_row, keys, values, lengths
):
    holding, rank_width, out_width = up.shape
    rows, width = hidden.shape
    cap = 2 * rows // replicas
    pieces = TILE // cap
    slots = replicas * TILE
    down_rows = jnp.swapaxes(down, 1, 2).reshape(holding * rank_width, width)
    up_rows = up.reshape(holding * rank_width, out_width)
    vmem = pl.BlockSpec(memory_space=pltpu.VMEM)
    hbm = pl.BlockSpec(memory_space=pl.ANY)
    return pl.pallas_call(
        functools.partial(kernel, replicas, holding, rank_width),
        out_shape=jax.ShapeDtypeStruct((rows, out_width), BF16),
        in_specs=[vmem] * 5 + [hbm] * 4,
        out_specs=vmem,
        scratch_shapes=[
            pltpu.VMEM(down_rows.shape, BF16),
            pltpu.VMEM(up_rows.shape, BF16),
            pltpu.VMEM(keys.shape, BF16),
            pltpu.VMEM(values.shape, BF16),
            pltpu.VMEM((replicas, TILE, width // pieces + LANES), BF16),
            pltpu.VMEM((replicas, TILE, width // pieces + LANES), BF16),
            pltpu.VMEM((slots, LANES), F32),
            pltpu.VMEM((slots, LANES), F32),
            pltpu.VMEM((replicas, TILE, out_width // pieces), BF16),
            pltpu.VMEM((replicas, TILE, out_width // pieces), BF16),
            pltpu.VMEM((rows, out_width), F32),
            pltpu.SemaphoreType.DMA((4,)),
            pltpu.SemaphoreType.DMA((replicas,)),
            pltpu.SemaphoreType.DMA((replicas,)),
            pltpu.SemaphoreType.DMA((2,)),
            pltpu.SemaphoreType.DMA((replicas,)),
            pltpu.SemaphoreType.DMA((replicas,)),
        ],
        compiler_params=pltpu.CompilerParams(
            collective_id=0, has_side_effects=True, vmem_limit_bytes=48 * 1024 * 1024
        ),
        name="adapter_attention",
    )(
        hidden, base, request_adapter.reshape(1, rows),
        adapter_pool_row.reshape(1, adapter_pool_row.shape[0]), lengths.reshape(1, rows),
        down_rows, up_rows, keys, values,
    )


def solution(mesh):
    return jax.shard_map(
        functools.partial(local_step, mesh.shape["replica"]),
        mesh=mesh,
        in_specs=(
            P(("groups", "replica"), "tensor"),
            P(("groups", "replica"), "tensor"),
            P(("groups", "replica"), "tensor", None),
            P(("groups", "replica"), None, "tensor"),
            P(("groups", "replica")),
            P("groups"),
            P(("groups", "replica"), None, "tensor"),
            P(("groups", "replica"), None, "tensor"),
            P(("groups", "replica")),
        ),
        out_specs=P(("groups", "replica"), "tensor"),
        check_vma=False,
    )
```

time: 152 us -> 41.4 us (0.27)
  waiting for transfers between devices: 101 us -> 0 us
  Pallas kernels: 0 us -> 33.2 us
  blocking collectives: 18.9 us -> 0 us
  between operations: 14.1 us -> 0.02 us
  matrix products: 13.9 us -> 0 us
  local copies, waits for them, and re-layouts: 2.38 us -> 7.95 us
  other arithmetic: 1.88 us -> 0 us
    reduce_scatter x1 -> x0, waiting for transfers between devices: 62.3 us -> none  [local(): lax.psum_scatter(jnp.dot(shrink, flattened_up_weight, preferred_element_t...]
    all_gather x1 -> x0, waiting for transfers between devices: 37.9 us -> none  [local(): lax.all_gather(hidden, 'replica', axis=0, tiled=True)]
    pallas_call x0 -> x1, Pallas kernels: none -> 33.2 us  [local_step(): pl.pallas_call(functools.partial(kernel, replicas, holding, rank_width),...]
    unnamed x1 -> x0, blocking collectives: 13.2 us -> none
    dot_general x2 -> x0, matrix products: 6.35 us -> none  [the longest x1 3.32 us: local(): jnp.dot(shrink, flattened_up_weight, preferred_element_type=jnp.float32)]
    psum x1 -> x0, blocking collectives: 5.72 us -> none  [local(): shrink = lax.psum(partial_value_sum, 'tensor').astype(jnp.bfloat16)]
    unnamed x11 -> x15, local copies, waits for them, and re-layouts: 2.38 us -> 7.95 us
    unnamed x1 -> x0, matrix products: 4.9 us -> none
  transfers between devices with their start and end apart: 2 -> 0, of which waited for: 2 -> 0; matrix products, arithmetic and copies ran while one was open for 2% -> 0% of each run, Pallas kernels for 0% -> 0%
where the time goes in v1:
time: 41.4 us; the launch traced here: 41.2 us
  Pallas kernels  33.2 us (80%)
  local copies, waits for them, and re-layouts  7.95 us (19%)
    pallas_call x1, Pallas kernels, local_step(): pl.pallas_call(functools.partial(kernel, replicas, holding, rank_width),...  33.2 us
    unnamed x15, local copies, waits for them, and re-layouts  7.95 us

profile of v1, /device:TPU:0, one launch (start us, length us, event | category | flops | bytes accessed | tf_op | source)
XLA Modules:
  0.0 41.2 jit_solution(16852017684001597499)
XLA Ops:
  0.0 0.0 copy-start
  0.0 1.9 %copy-done = bf16[32,192,256]{2,1,0:T(8,128)(2,1)S(1)} copy-done((bf16[32,192,256]{2,1,0:T(8,128)(2,1)S(1)}, bf16[32,192,256]{2,1,0:T(8,128)(2,1)}, u32[]{:S(2)}) %copy-start) | copy-done | bytes 3145752
  1.9 0.0 copy-start.1
  1.9 1.6 %copy-done.1 = bf16[8,64,2048]{2,1,0:T(8,128)(2,1)S(1)} copy-done((bf16[8,64,2048]{2,1,0:T(8,128)(2,1)S(1)}, bf16[8,64,2048]{2,1,0:T(8,128)(2,1)}, u32[]{:S(2)}) %copy-start.1) | copy-done | bytes 2097176
  3.5 0.0 copy-start.2
  3.5 0.9 %copy-done.2 = bf16[32,4096]{1,0:T(8,128)(2,1)S(1)} copy-done((bf16[32,4096]{1,0:T(8,128)(2,1)S(1)}, bf16[32,4096]{1,0:T(8,128)(2,1)}, u32[]{:S(2)}) %copy-start.2) | copy-done | bytes 262168
  4.4 0.0 copy-start.3
  4.4 0.9 %copy-done.3 = bf16[32,2048]{1,0:T(8,128)(2,1)S(1)} copy-done((bf16[32,2048]{1,0:T(8,128)(2,1)S(1)}, bf16[32,2048]{1,0:T(8,128)(2,1)}, u32[]{:S(2)}) %copy-start.3) | copy-done | bytes 131096
  5.3 0.0 copy-start.4
  5.3 0.7 %copy-done.4 = s32[32]{0:T(128)S(1)} copy-done((s32[32]{0:T(128)S(1)}, s32[32]{0:T(128)}, u32[]{:S(2)}) %copy-start.4) | copy-done | bytes 152
  6.0 0.0 copy-start.5
  6.0 0.7 %copy-done.5 = s32[64]{0:T(128)S(1)} copy-done((s32[64]{0:T(128)S(1)}, s32[64]{0:T(128)}, u32[]{:S(2)}) %copy-start.5) | copy-done | bytes 280
  6.6 0.0 copy-start.6
  6.7 0.7 %copy-done.6 = s32[32]{0:T(128)S(1)} copy-done((s32[32]{0:T(128)S(1)}, s32[32]{0:T(128)}, u32[]{:S(2)}) %copy-start.6) | copy-done | bytes 152
  7.3 33.2 %adapter_attention.1 = bf16[32,2048]{1,0:T(8,128)(2,1)S(1)} custom-call(bf16[32,4096]{1,0:T(8,128)(2,1)S(1)} %copy-done.2, bf16[32,2048]{1,0:T(8,128)(2,1)S(1)} %copy-done.3, s32[1,32]{1,0:T(1,128)S(1)} %bitcast.8, s32[1,64]{1,0:T(1,128)S(1)} %bitcast.9, s32[1,32]{1,0:T(1,128)S(1)} %bitcast.10, bf16[512,4096]{1,0:T(8,128)(2,1)} %bitcast.11, ...), custom_call_target="tpu_custom_call" | custom-call | tf_op jit(solution)/shard_map/adapter_attention/pallas_call | solution.py:261
  40.5 0.7 %copy.11 = bf16[32,2048]{1,0:T(8,128)(2,1)} copy(bf16[32,2048]{1,0:T(8,128)(2,1)S(1)} %adapter_attention.1) | data formatting | bytes 262144
Async XLA Ops:
  0.0 1.9 %copy-start = (bf16[32,192,256]{2,1,0:T(8,128)(2,1)S(1)}, bf16[32,192,256]{2,1,0:T(8,128)(2,1)}, u32[]{:S(2)}) copy-start(bf16[32,192,256]{2,1,0:T(8,128)(2,1)} %key_hbm.1) | copy-start | bytes 9437188
  1.9 1.6 %copy-start.1 = (bf16[8,64,2048]{2,1,0:T(8,128)(2,1)S(1)}, bf16[8,64,2048]{2,1,0:T(8,128)(2,1)}, u32[]{:S(2)}) copy-start(bf16[8,64,2048]{2,1,0:T(8,128)(2,1)} %param.12) | copy-start | bytes 6291460
  3.5 0.9 %copy-start.2 = (bf16[32,4096]{1,0:T(8,128)(2,1)S(1)}, bf16[32,4096]{1,0:T(8,128)(2,1)}, u32[]{:S(2)}) copy-start(bf16[32,4096]{1,0:T(8,128)(2,1)} %hidden_ref.1) | copy-start | bytes 786436
  4.4 0.9 %copy-start.3 = (bf16[32,2048]{1,0:T(8,128)(2,1)S(1)}, bf16[32,2048]{1,0:T(8,128)(2,1)}, u32[]{:S(2)}) copy-start(bf16[32,2048]{1,0:T(8,128)(2,1)} %base_ref.1) | copy-start | bytes 393220
  5.3 0.7 %copy-start.4 = (s32[32]{0:T(128)S(1)}, s32[32]{0:T(128)}, u32[]{:S(2)}) copy-start(s32[32]{0:T(128)} %param.13) | copy-start | bytes 388
  6.0 0.7 %copy-start.5 = (s32[64]{0:T(128)S(1)}, s32[64]{0:T(128)}, u32[]{:S(2)}) copy-start(s32[64]{0:T(128)} %param.14) | copy-start | bytes 772
  6.6 0.7 %copy-start.6 = (s32[32]{0:T(128)S(1)}, s32[32]{0:T(128)}, u32[]{:S(2)}) copy-start(s32[32]{0:T(128)} %param.17) | copy-start | bytes 388

commit v2 on v1

--- a/solution.py
+++ b/solution.py
@@ -283,7 +283,7 @@
             pltpu.SemaphoreType.DMA((replicas,)),
         ],
         compiler_params=pltpu.CompilerParams(
-            collective_id=0, has_side_effects=True, vmem_limit_bytes=48 * 1024 * 1024
+            collective_id=0, has_side_effects=True, vmem_limit_bytes=63 * 1024 * 1024
         ),
         name="adapter_attention",
     )(

time: 41.4 us -> 36.6 us (0.88)
  local copies, waits for them, and re-layouts: 7.95 us -> 1.57 us
  Pallas kernels: 33.2 us -> 34.9 us
    unnamed x15 -> x1, local copies, waits for them, and re-layouts: 7.95 us -> 1.57 us
    pallas_call x1, Pallas kernels: 33.2 us -> 34.9 us  [local_step(): pl.pallas_call(functools.partial(kernel, replicas, holding, rank_width),...]
where the time goes in v2:
time: 36.6 us; the launch traced here: 36.4 us
  Pallas kernels  34.9 us (95%)
  local copies, waits for them, and re-layouts  1.57 us (4%)
    pallas_call x1, Pallas kernels, local_step(): pl.pallas_call(functools.partial(kernel, replicas, holding, rank_width),...  34.9 us
    unnamed x1, local copies, waits for them, and re-layouts  1.57 us

profile of v2, /device:TPU:0, one launch (start us, length us, event | category | flops | bytes accessed | tf_op | source)
XLA Modules:
  0.0 36.4 jit_solution(6424751225874953814)
XLA Ops:
  0.0 34.9 %adapter_attention.1 = bf16[32,2048]{1,0:T(8,128)(2,1)} custom-call(bf16[32,4096]{1,0:T(8,128)(2,1)} %hidden_ref.1, bf16[32,2048]{1,0:T(8,128)(2,1)} %base_ref.1, s32[1,32]{1,0:T(1,128)} %bitcast.9, s32[1,64]{1,0:T(1,128)} %bitcast.10, s32[1,32]{1,0:T(1,128)} %bitcast.11, bf16[512,4096]{1,0:T(8,128)(2,1)} %bitcast.7, bf16[512,2048]{1,0:T(8,128)(2,1)} %bitcast.8, ...), custom_call_target="tpu_custom_call" | custom-call | tf_op jit(solution)/shard_map/adapter_attention/pallas_call | solution.py:261
  34.9 1.6 %copy.11 = bf16[32,2048]{1,0:T(8,128)(2,1)} copy(bf16[32,2048]{1,0:T(8,128)(2,1)} %adapter_attention.1) | data formatting | bytes 262144

commit v3 on v2

--- a/solution.py
+++ b/solution.py
@@ -10,6 +10,7 @@
 HEAD_WIDTH = 128
 TILE = 16
 LANES = 128
+PARTS = 2
 F32 = jnp.float32
 BF16 = jnp.bfloat16
 
@@ -39,7 +40,8 @@
 ):
     rows, width = hidden_ref.shape
     out_width = up.shape[1]
-    cap = 2 * rows // replicas
+    parts = send_rows.shape[0]
+    cap = 2 * rows // replicas // parts
     pieces = TILE // cap
     slots = replicas * TILE
     piece_width = width // pieces
@@ -81,120 +83,154 @@
     place_row = jnp.sum(jnp.where(same & before_j, 1, 0), axis=0, keepdims=True)
 
     at_row = iota((slots, rows), 0)
-    pick = (owner_row == at_row // TILE) & (place_row == at_row % cap)
-    pick_bf = jnp.where(pick, 1.0, 0.0).astype(BF16)
-    local_slot = jnp.sum(jnp.where(pick, local_row + 1, 0), axis=1, keepdims=True) - 1
     piece_of = (iota((slots, 1), 0) % TILE) // cap
-
     step = min(piece_width, 512)
-    for start in range(0, piece_width, step):
-        taken = None
-        for h in range(pieces):
-            found = jnp.dot(
-                pick_bf, hidden_ref[:, h * piece_width + start:h * piece_width + start + step],
-                preferred_element_type=F32,
-            )
-            taken = found if taken is None else jnp.where(piece_of == h, found, taken)
-        send_rows[:, :, start:start + step] = taken.astype(BF16).reshape(replicas, TILE, step)
-    send_rows[:, :, piece_width:] = jnp.broadcast_to(
-        local_slot.astype(F32), (slots, LANES)
-    ).astype(BF16).reshape(replicas, TILE, LANES)
-
-    pl.semaphore_wait(barrier, replicas)
-
-    def exchange(source, target, send_sem, recv_sem):
+
+    def fill(number):
+        pick = (owner_row == at_row // TILE) & (place_row == at_row % cap + number * cap)
+        pick_pieces = jnp.concatenate(
+            [
+                jnp.where(pick & ((at_row % TILE) // cap == h), 1.0, 0.0).astype(BF16)
+                for h in range(pieces)
+            ],
+            axis=1,
+        )
+        local_slot = jnp.sum(jnp.where(pick, local_row + 1, 0), axis=1, keepdims=True) - 1
+        for start in range(0, piece_width, step):
+            stacked = jnp.concatenate(
+                [
+                    hidden_ref[:, h * piece_width + start:h * piece_width + start + step]
+                    for h in range(pieces)
+                ],
+                axis=0,
+            )
+            taken = jnp.dot(pick_pieces, stacked, preferred_element_type=F32)
+            send_rows[number, :, :, start:start + step] = taken.astype(BF16).reshape(
+                replicas, TILE, step
+            )
+        send_rows[number, :, :, piece_width:] = jnp.broadcast_to(
+            local_slot.astype(F32), (slots, LANES)
+        ).astype(BF16).reshape(replicas, TILE, LANES)
+
+    def exchange(number, source, target, send_sem, recv_sem):
         copies = []
         order = sorted(range(1, replicas), key=lambda off: abs(off - replicas // 2))
         for off in order:
             there = lax.rem(me + off, replicas)
             copy = pltpu.make_async_remote_copy(
-                src_ref=source.at[there], dst_ref=target.at[me],
-                send_sem=send_sem.at[off], recv_sem=recv_sem.at[off],
+                src_ref=source.at[number, there], dst_ref=target.at[number, me],
+                send_sem=send_sem.at[number, off], recv_sem=recv_sem.at[number, off],
                 device_id={"replica": there}, device_id_type=pl.DeviceIdType.MESH,
             )
             copy.start()
             copies.append(copy)
+        target[number, me] = source[number, me]
         return copies
 
-    row_copies = exchange(send_rows, got_rows, row_send, row_recv)
-    got_rows[me] = send_rows[me]
-    loads[0].wait()
-    for copy in row_copies:
-        copy.wait()
-
-    partial_sum = None
-    for h in range(pieces):
-        term = lax.dot_general(
-            got_rows[:, :, :piece_width].reshape(slots, piece_width),
-            down[:, h * piece_width:(h + 1) * piece_width],
-            (((1,), (1,)), ((), ())), preferred_element_type=F32,
-        )
-        partial_sum = term if partial_sum is None else jnp.where(piece_of == h, term, partial_sum)
-    local = got_rows[:, :, piece_width:].reshape(slots, LANES).astype(F32)
     per_tile = LANES // rank_width
     tiles = holding * rank_width // LANES
     lane_adapter = (iota((slots, LANES), 1) // rank_width).astype(F32)
-    folded = jnp.zeros((slots, LANES), F32)
-    for tile in range(tiles):
-        keep = local == lane_adapter + tile * per_tile
-        folded += jnp.where(keep, partial_sum[:, tile * LANES:(tile + 1) * LANES], 0.0)
-    shift = rank_width
-    while shift < LANES:
-        folded = folded + pltpu.roll(folded, shift, 1)
-        shift *= 2
-    shift = cap
     row_at = iota((slots, 1), 0)
-    while shift < TILE:
-        upper = (row_at // shift) % 2 == 1
-        folded = folded + jnp.where(
-            upper, pltpu.roll(folded, shift, 0), pltpu.roll(folded, slots - shift, 0)
-        )
-        shift *= 2
-    part[...] = folded
-    swap = pltpu.make_async_remote_copy(
-        src_ref=part, dst_ref=other_part, send_sem=part_sem.at[0], recv_sem=part_sem.at[1],
-        device_id={"tensor": 1 - core}, device_id_type=pl.DeviceIdType.MESH,
-    )
-    swap.start()
-    loads[1].wait()
-    swap.wait()
-    shrink = (part[...] + other_part[...]).astype(BF16).astype(F32)
-    wide = jnp.concatenate(
-        [
-            jnp.where(local == lane_adapter + tile * per_tile, shrink, 0.0).astype(BF16)
-            for tile in range(tiles)
-        ],
-        axis=1,
-    )
-    step = min(delta_width, 512)
-    for start in range(0, delta_width, step):
-        taken = None
+
+    def shrink_part(number):
+        partial_sum = None
         for h in range(pieces):
-            found = jnp.dot(
-                wide, up[:, h * delta_width + start:h * delta_width + start + step],
-                preferred_element_type=F32,
-            )
-            taken = found if taken is None else jnp.where(piece_of == h, found, taken)
-        send_delta[:, :, start:start + step] = taken.astype(BF16).reshape(replicas, TILE, step)
-    delta_copies = exchange(send_delta, got_delta, delta_send, delta_recv)
-    got_delta[me] = send_delta[me]
+            term = lax.dot_general(
+                got_rows[number, :, :, :piece_width].reshape(slots, piece_width),
+                down[:, h * piece_width:(h + 1) * piece_width],
+                (((1,), (1,)), ((), ())), preferred_element_type=F32,
+            )
+            partial_sum = (
+                term if partial_sum is None else jnp.where(piece_of == h, term, partial_sum)
+            )
+        local = got_rows[number, :, :, piece_width:].reshape(slots, LANES).astype(F32)
+        folded = jnp.zeros((slots, LANES), F32)
+        for tile in range(tiles):
+            keep = local == lane_adapter + tile * per_tile
+            folded += jnp.where(keep, partial_sum[:, tile * LANES:(tile + 1) * LANES], 0.0)
+        shift = rank_width
+        while shift < LANES:
+            folded = folded + pltpu.roll(folded, shift, 1)
+            shift *= 2
+        shift = cap
+        while shift < TILE:
+            upper = (row_at // shift) % 2 == 1
+            folded = folded + jnp.where(
+                upper, pltpu.roll(folded, shift, 0), pltpu.roll(folded, slots - shift, 0)
+            )
+            shift *= 2
+        part[number] = folded
+        swap = pltpu.make_async_remote_copy(
+            src_ref=part.at[number], dst_ref=other_part.at[number],
+            send_sem=part_sem.at[number, 0], recv_sem=part_sem.at[number, 1],
+            device_id={"tensor": 1 - core}, device_id_type=pl.DeviceIdType.MESH,
+        )
+        swap.start()
+        return swap
+
+    def expand_part(number):
+        local = got_rows[number, :, :, piece_width:].reshape(slots, LANES).astype(F32)
+        shrink = (part[number] + other_part[number]).astype(BF16).astype(F32)
+        wide = jnp.concatenate(
+            [
+                jnp.where(local == lane_adapter + tile * per_tile, shrink, 0.0).astype(BF16)
+                for tile in range(tiles)
+            ],
+            axis=1,
+        )
+        wide_step = min(delta_width, 512)
+        for start in range(0, delta_width, wide_step):
+            taken = None
+            for h in range(pieces):
+                found = jnp.dot(
+                    wide, up[:, h * delta_width + start:h * delta_width + start + wide_step],
+                    preferred_element_type=F32,
+                )
+                taken = found if taken is None else jnp.where(piece_of == h, found, taken)
+            send_delta[number, :, :, start:start + wide_step] = taken.astype(BF16).reshape(
+                replicas, TILE, wide_step
+            )
+
+    fill(0)
+    pl.semaphore_wait(barrier, replicas)
+    row_copies = []
+    for number in range(parts):
+        if number:
+            fill(number)
+        row_copies.append(exchange(number, send_rows, got_rows, row_send, row_recv))
+    delta_copies, swaps = [], []
+    for number in range(parts):
+        for copy in row_copies[number]:
+            copy.wait_recv()
+        if number == 0:
+            loads[0].wait()
+        swap = shrink_part(number)
+        if number == 0:
+            loads[1].wait()
+        swap.wait_recv()
+        swaps.append(swap)
+        expand_part(number)
+        delta_copies.append(exchange(number, send_delta, got_delta, delta_send, delta_recv))
 
     at_col = iota((rows, slots), 1)
-    mine = (owner_col == at_col // TILE) & (place_col == at_col % cap)
-    back = [
-        jnp.where(mine & ((at_col % TILE) // cap == h), 1.0, 0.0).astype(BF16)
-        for h in range(pieces)
-    ]
     loads[2].wait()
     loads[3].wait()
-    for copy in delta_copies:
-        copy.wait()
+    deltas = [None] * pieces
+    for number in range(parts):
+        mine = (owner_col == at_col // TILE) & (place_col == at_col % cap + number * cap)
+        for copy in delta_copies[number]:
+            copy.wait_recv()
+        for h in range(pieces):
+            back = jnp.where(mine & ((at_col % TILE) // cap == h), 1.0, 0.0).astype(BF16)
+            found = jnp.dot(
+                back, got_delta[number].reshape(slots, delta_width), preferred_element_type=F32
+            )
+            deltas[h] = found if deltas[h] is None else deltas[h] + found
     for h in range(pieces):
         columns = slice(h * delta_width, (h + 1) * delta_width)
-        delta = jnp.dot(
-            back[h], got_delta[...].reshape(slots, delta_width), preferred_element_type=F32
-        )
-        query[:, columns] = (base_ref[:, columns].astype(F32) + delta).astype(BF16).astype(F32)
+        query[:, columns] = (base_ref[:, columns].astype(F32) + deltas[h]).astype(BF16).astype(F32)
+    for copy in sum(row_copies, []) + sum(delta_copies, []) + swaps:
+        copy.wait_send()
 
     cache_len, kv_width = keys.shape[1:]
     kv_heads = kv_width // HEAD_WIDTH
@@ -251,7 +287,8 @@
 ):
     holding, rank_width, out_width = up.shape
     rows, width = hidden.shape
-    cap = 2 * rows // replicas
+    parts = min(PARTS, 2 * rows // replicas)
+    cap = 2 * rows // replicas // parts
     pieces = TILE // cap
     slots = replicas * TILE
     down_rows = jnp.swapaxes(down, 1, 2).reshape(holding * rank_width, width)
@@ -268,19 +305,19 @@
             pltpu.VMEM(up_rows.shape, BF16),
             pltpu.VMEM(keys.shape, BF16),
             pltpu.VMEM(values.shape, BF16),
-            pltpu.VMEM((replicas, TILE, width // pieces + LANES), BF16),
-            pltpu.VMEM((replicas, TILE, width // pieces + LANES), BF16),
-            pltpu.VMEM((slots, LANES), F32),
-            pltpu.VMEM((slots, LANES), F32),
-            pltpu.VMEM((replicas, TILE, out_width // pieces), BF16),
-            pltpu.VMEM((replicas, TILE, out_width // pieces), BF16),
+            pltpu.VMEM((parts, replicas, TILE, width // pieces + LANES), BF16),
+            pltpu.VMEM((parts, replicas, TILE, width // pieces + LANES), BF16),
+            pltpu.VMEM((parts, slots, LANES), F32),
+            pltpu.VMEM((parts, slots, LANES), F32),
+            pltpu.VMEM((parts, replicas, TILE, out_width // pieces), BF16),
+            pltpu.VMEM((parts, replicas, TILE, out_width // pieces), BF16),
             pltpu.VMEM((rows, out_width), F32),
             pltpu.SemaphoreType.DMA((4,)),
-            pltpu.SemaphoreType.DMA((replicas,)),
-            pltpu.SemaphoreType.DMA((replicas,)),
-            pltpu.SemaphoreType.DMA((2,)),
-            pltpu.SemaphoreType.DMA((replicas,)),
-            pltpu.SemaphoreType.DMA((replicas,)),
+            pltpu.SemaphoreType.DMA((parts, replicas)),
+            pltpu.SemaphoreType.DMA((parts, replicas)),
+            pltpu.SemaphoreType.DMA((parts, 2)),
+            pltpu.SemaphoreType.DMA((parts, replicas)),
+            pltpu.SemaphoreType.DMA((parts, replicas)),
         ],
         compiler_params=pltpu.CompilerParams(
             collective_id=0, has_side_effects=True, vmem_limit_bytes=63 * 1024 * 1024

time: 36.6 us -> 36.4 us (level)
  no operation moved by 1% of the time
where the time goes in v3:
time: 36.4 us; the launch traced here: 36.2 us
  Pallas kernels  34.7 us (95%)
  local copies, waits for them, and re-layouts  1.57 us (4%)
    pallas_call x1, Pallas kernels, local_step(): pl.pallas_call(functools.partial(kernel, replicas, holding, rank_width),...  34.7 us
    unnamed x1, local copies, waits for them, and re-layouts  1.57 us

profile of v3, /device:TPU:0, one launch (start us, length us, event | category | flops | bytes accessed | tf_op | source)
XLA Modules:
  0.0 36.2 jit_solution(10645761376413035598)
XLA Ops:
  0.0 34.7 %adapter_attention.1 = bf16[32,2048]{1,0:T(8,128)(2,1)} custom-call(bf16[32,4096]{1,0:T(8,128)(2,1)} %hidden_ref.1, bf16[32,2048]{1,0:T(8,128)(2,1)} %base_ref.1, s32[1,32]{1,0:T(1,128)} %bitcast.9, s32[1,64]{1,0:T(1,128)} %bitcast.10, s32[1,32]{1,0:T(1,128)} %bitcast.11, bf16[512,4096]{1,0:T(8,128)(2,1)} %bitcast.7, bf16[512,2048]{1,0:T(8,128)(2,1)} %bitcast.8, ...), custom_call_target="tpu_custom_call" | custom-call | tf_op jit(solution)/shard_map/adapter_attention/pallas_call | solution.py:298
  34.7 1.6 %copy.11 = bf16[32,2048]{1,0:T(8,128)(2,1)} copy(bf16[32,2048]{1,0:T(8,128)(2,1)} %adapter_attention.1) | data formatting | bytes 262144

commit v4 on v3

--- a/solution.py
+++ b/solution.py
@@ -10,7 +10,7 @@
 HEAD_WIDTH = 128
 TILE = 16
 LANES = 128
-PARTS = 2
+PARTS = 1
 F32 = jnp.float32
 BF16 = jnp.bfloat16
 
@@ -112,19 +112,26 @@
             local_slot.astype(F32), (slots, LANES)
         ).astype(BF16).reshape(replicas, TILE, LANES)
 
-    def exchange(number, source, target, send_sem, recv_sem):
+    half = piece_width // 2
+    spans = ((0, half), (half, piece_width + LANES))
+
+    def exchange(number, source, target, send_sem, recv_sem, span=None, lane=None):
         copies = []
-        order = sorted(range(1, replicas), key=lambda off: abs(off - replicas // 2))
+        lane = number if lane is None else lane
+        span = (0, source.shape[3]) if span is None else span
+        columns = slice(*span)
+        order = sorted(range(1, replicas), key=lambda off: -abs(off - replicas // 2))
         for off in order:
             there = lax.rem(me + off, replicas)
             copy = pltpu.make_async_remote_copy(
-                src_ref=source.at[number, there], dst_ref=target.at[number, me],
-                send_sem=send_sem.at[number, off], recv_sem=recv_sem.at[number, off],
+                src_ref=source.at[number, there, :, columns],
+                dst_ref=target.at[number, me, :, columns],
+                send_sem=send_sem.at[lane, off], recv_sem=recv_sem.at[lane, off],
                 device_id={"replica": there}, device_id_type=pl.DeviceIdType.MESH,
             )
             copy.start()
             copies.append(copy)
-        target[number, me] = source[number, me]
+        target[number, me, :, columns] = source[number, me, :, columns]
         return copies
 
     per_tile = LANES // rank_width
@@ -133,16 +140,20 @@
     row_at = iota((slots, 1), 0)
 
     def shrink_part(number):
-        partial_sum = None
-        for h in range(pieces):
-            term = lax.dot_general(
-                got_rows[number, :, :, :piece_width].reshape(slots, piece_width),
-                down[:, h * piece_width:(h + 1) * piece_width],
-                (((1,), (1,)), ((), ())), preferred_element_type=F32,
-            )
-            partial_sum = (
-                term if partial_sum is None else jnp.where(piece_of == h, term, partial_sum)
-            )
+        terms = [None] * pieces
+        for at, span in enumerate(((0, half), (half, piece_width))):
+            for copy in row_copies[2 * number + at]:
+                copy.wait_recv()
+            for h in range(pieces):
+                term = lax.dot_general(
+                    got_rows[number, :, :, span[0]:span[1]].reshape(slots, half),
+                    down[:, h * piece_width + span[0]:h * piece_width + span[1]],
+                    (((1,), (1,)), ((), ())), preferred_element_type=F32,
+                )
+                terms[h] = term if terms[h] is None else terms[h] + term
+        partial_sum = terms[0]
+        for h in range(1, pieces):
+            partial_sum = jnp.where(piece_of == h, terms[h], partial_sum)
         local = got_rows[number, :, :, piece_width:].reshape(slots, LANES).astype(F32)
         folded = jnp.zeros((slots, LANES), F32)
         for tile in range(tiles):
@@ -197,11 +208,12 @@
     for number in range(parts):
         if number:
             fill(number)
-        row_copies.append(exchange(number, send_rows, got_rows, row_send, row_recv))
+        for at, span in enumerate(spans):
+            row_copies.append(
+                exchange(number, send_rows, got_rows, row_send, row_recv, span, 2 * number + at)
+            )
     delta_copies, swaps = [], []
     for number in range(parts):
-        for copy in row_copies[number]:
-            copy.wait_recv()
         if number == 0:
             loads[0].wait()
         swap = shrink_part(number)
@@ -313,8 +325,8 @@
             pltpu.VMEM((parts, replicas, TILE, out_width // pieces), BF16),
             pltpu.VMEM((rows, out_width), F32),
             pltpu.SemaphoreType.DMA((4,)),
-            pltpu.SemaphoreType.DMA((parts, replicas)),
-            pltpu.SemaphoreType.DMA((parts, replicas)),
+            pltpu.SemaphoreType.DMA((2 * parts, replicas)),
+            pltpu.SemaphoreType.DMA((2 * parts, replicas)),
             pltpu.SemaphoreType.DMA((parts, 2)),
             pltpu.SemaphoreType.DMA((parts, replicas)),
             pltpu.SemaphoreType.DMA((parts, replicas)),

time: 36.4 us -> 34.3 us (0.942)
  the two profiles are of different devices: /device:TPU:0 before, /device:TPU:7 now
where the time goes in v4:
time: 34.3 us; the launch traced here: 34.2 us
  Pallas kernels  32.6 us (95%)
  local copies, waits for them, and re-layouts  1.57 us (5%)
    pallas_call x1, Pallas kernels, local_step(): pl.pallas_call(functools.partial(kernel, replicas, holding, rank_width),...  32.6 us
    unnamed x1, local copies, waits for them, and re-layouts  1.57 us

profile of v4, /device:TPU:7, one launch (start us, length us, event | category | flops | bytes accessed | tf_op | source)
XLA Modules:
  0.0 34.2 jit_solution(10736116412688409999)
XLA Ops:
  0.0 32.6 %adapter_attention.1 = bf16[32,2048]{1,0:T(8,128)(2,1)} custom-call(bf16[32,4096]{1,0:T(8,128)(2,1)} %hidden_ref.1, bf16[32,2048]{1,0:T(8,128)(2,1)} %base_ref.1, s32[1,32]{1,0:T(1,128)} %bitcast.9, s32[1,64]{1,0:T(1,128)} %bitcast.10, s32[1,32]{1,0:T(1,128)} %bitcast.11, bf16[512,4096]{1,0:T(8,128)(2,1)} %bitcast.7, bf16[512,2048]{1,0:T(8,128)(2,1)} %bitcast.8, ...), custom_call_target="tpu_custom_call" | custom-call | tf_op jit(solution)/shard_map/adapter_attention/pallas_call | solution.py:310
  32.6 1.6 %copy.11 = bf16[32,2048]{1,0:T(8,128)(2,1)} copy(bf16[32,2048]{1,0:T(8,128)(2,1)} %adapter_attention.1) | data formatting | bytes 262144
